TPU v7x, 256 devices: a whole 4x4x8 slice. The times are simulated.
256 devices in a mesh: seq: 32 (over x, y, core), head: 8 (over z).
Axes of the slice: x: 4, y: 4, z: 8, core: 2. Of those that a mesh axis runs over, the one named last changes fastest.
Arguments:
- hidden_in: bfloat16 [16384, 2048], P('seq', 'head'), may hold values from -8 to 8
- proj_weight: bfloat16 [2048, 10240], P(None, 'head'), may hold values from -0.125 to 0.125
- beta_weight: bfloat16 [2048, 32], P(None, 'head'), may hold values from -1 to 1
- norm_gain: float32 [2048], P('head'), may hold values from 0.1 to 1.9
- out_weight: bfloat16 [2048, 2048], P('head'), may hold values from -0.125 to 0.125
- cotangent: bfloat16 [16384, 2048], P('seq', 'head'), may hold values from -6 to 6
Outputs:
- mixed_out: bfloat16 [16384, 2048], P('seq', 'head')
- grad_input: bfloat16 [16384, 2048], P('seq', 'head')
All inputs are finite; a program needn't handle non-finite values.
Results may differ from a plain program's by a relative error of at most 0.02.
Values may be sent and summed in bfloat16 or wider, within the bound.
A program may use at most 128 MiB of HBM per device.

v0:
```python
from functools import partial
import jax
import jax.numpy as jnp
from jax import lax
from jax.sharding import PartitionSpec as P

DK = 128
REFL = 2
HIGHEST = lax.Precision.HIGHEST


def passed_along(shard, axis, by):
    size = lax.axis_size(axis)
    pairs = [(i, i + by) for i in range(size) if 0 <= i + by < size]
    return lax.ppermute(shard, axis, pairs)


def product(left, right):
    return jnp.matmul(left, right, precision=HIGHEST)


def unit_rows(vectors):
    return vectors / jnp.sqrt(jnp.sum(vectors * vectors, axis=-1, keepdims=True) + 1e-06)


def solve_lower(matrix, target):
    return jax.scipy.linalg.solve_triangular(matrix, target, lower=True, unit_diagonal=True)


def prepare_head(projected, beta_logits, block_size):
    row_count = projected.shape[0]
    key_width = projected.shape[1] // (1 + 2 * REFL)
    blocks = row_count // block_size
    pair_span = block_size * REFL
    pieces = projected.reshape(row_count, 1 + 2 * REFL, key_width)
    queries = unit_rows(pieces[:, 0]).reshape(blocks, block_size, key_width)
    key_rows = unit_rows(pieces[:, 1 : 1 + REFL]).reshape(blocks, pair_span, key_width)
    values = pieces[:, 1 + REFL :].reshape(blocks, pair_span, key_width)
    strength = (2.0 * jax.nn.sigmoid(beta_logits)).reshape(blocks, pair_span, 1)
    strict_below = jnp.arange(pair_span)[:, None] > jnp.arange(pair_span)[None, :]
    key_gram = strength * product(key_rows, jnp.swapaxes(key_rows, 1, 2))
    lower_unit = jnp.where(strict_below, key_gram, 0.0) + jnp.eye(pair_span, dtype=jnp.float32)
    target = strength * jnp.concatenate([values, key_rows], axis=2)
    solved = jax.vmap(solve_lower)(lower_unit, target)
    return (queries, key_rows, solved[:, :, key_width:], solved[:, :, :key_width])


def compose_head(key_rows, shifts, updates):
    key_width = key_rows.shape[2]
    identity = jnp.eye(key_width, dtype=jnp.float32)
    trans_all = identity - product(jnp.swapaxes(key_rows, 1, 2), shifts)
    writes = product(jnp.swapaxes(key_rows, 1, 2), updates)

    def absorb(state_pair, block_pair):
        return (
            (
                product(block_pair[0], state_pair[0]),
                product(block_pair[0], state_pair[1]) + block_pair[1],
            ),
            None,
        )

    result, _ = lax.scan(absorb, (identity, jnp.zeros_like(identity)), (trans_all, writes))
    return result


def read_head(queries, key_rows, shifts, updates, start_state, gain_row):
    block_size = queries.shape[1]
    pair_span = key_rows.shape[1]
    visible = jnp.arange(pair_span)[None, :] <= REFL * jnp.arange(block_size)[:, None] + REFL - 1

    def advance(memory, block_items):
        query_blk, key_blk, shift_blk, update_blk = block_items
        corrected = update_blk - product(shift_blk, memory)
        scores = jnp.where(visible, product(query_blk, key_blk.T), 0.0)
        output = product(query_blk, memory) + product(scores, corrected)
        return (memory + product(key_blk.T, corrected), output)

    _, outputs = lax.scan(advance, start_state, (queries, key_rows, shifts, updates))
    outputs = outputs.reshape(-1, outputs.shape[2])
    inverse_rms = lax.rsqrt(jnp.mean(outputs * outputs, axis=-1, keepdims=True) + 1e-05)
    return outputs * inverse_rms * gain_row


def local(hidden_in, proj_weight, beta_weight, norm_gain, out_weight, cotangent):
    row_count = hidden_in.shape[0]
    block_size = min(64, row_count)
    head_count = norm_gain.shape[0] // DK
    head_width = proj_weight.shape[1] // head_count
    contract = (((1,), (1,)), ((), ()))
    hidden_part = lax.all_gather(hidden_in, "head", axis=1, tiled=True)
    cot_part = lax.all_gather(cotangent, "head", axis=1, tiled=True)
    projected = jnp.dot(hidden_part, proj_weight, preferred_element_type=jnp.float32)
    beta_logits = jnp.dot(hidden_part, beta_weight, preferred_element_type=jnp.float32)
    dnormed = lax.dot_general(cot_part, out_weight, contract, preferred_element_type=jnp.float32)
    projected, beta_logits, dnormed = (projected, beta_logits, dnormed)
    proj_heads = jnp.moveaxis(projected.reshape(row_count, head_count, head_width), 1, 0)
    logit_heads = jnp.moveaxis(beta_logits.reshape(row_count, head_count, REFL), 1, 0)
    gain_heads = norm_gain.reshape(head_count, DK)
    prepared, prep_pull = jax.vjp(
        jax.vmap(partial(prepare_head, block_size=block_size)), proj_heads, logit_heads
    )
    (transit, offset), compose_pull = jax.vjp(
        jax.vmap(compose_head), prepared[1], prepared[2], prepared[3]
    )
    turn_count = lax.axis_size("seq") - 1

    def forward_turn(turn_index, state_pair):
        incoming = passed_along(state_pair[1], "seq", 1)
        return (incoming, product(transit, incoming) + offset)

    start_state, _ = lax.fori_loop(0, turn_count, forward_turn, (jnp.zeros_like(offset), offset))

    def read_all(queries, key_rows, shifts, updates, memory):
        return jax.vmap(read_head)(queries, key_rows, shifts, updates, memory, gain_heads)

    normed, read_pull = jax.vjp(
        read_all, prepared[0], prepared[1], prepared[2], prepared[3], start_state
    )
    normed_rows = (
        jnp.moveaxis(normed, 0, 1).reshape(row_count, head_count * DK).astype(jnp.bfloat16)
    )
    mixed_terms = jnp.dot(normed_rows, out_weight, preferred_element_type=jnp.float32)
    mixed_out = lax.psum_scatter(
        mixed_terms.astype(jnp.bfloat16), "head", scatter_dimension=1, tiled=True
    )
    dnormed_heads = jnp.moveaxis(dnormed.reshape(row_count, head_count, DK), 1, 0)
    grad_query, grad_keys, grad_shifts, grad_updates, grad_start = read_pull(dnormed_heads)
    transit_back = jnp.swapaxes(transit, 1, 2)

    def backward_turn(turn_index, state_pair):
        arriving = passed_along(state_pair[1], "seq", -1)
        return (arriving, grad_start + product(transit_back, arriving))

    after_grad, _ = lax.fori_loop(
        0, turn_count, backward_turn, (jnp.zeros_like(grad_start), grad_start)
    )
    keys_extra, shifts_extra, updates_extra = compose_pull(
        (product(after_grad, jnp.swapaxes(start_state, 1, 2)), after_grad)
    )
    grad_proj, grad_logit = prep_pull(
        (
            grad_query,
            grad_keys + keys_extra,
            grad_shifts + shifts_extra,
            grad_updates + updates_extra,
        )
    )
    proj_back = (
        jnp.moveaxis(grad_proj, 0, 1)
        .reshape(row_count, head_count * head_width)
        .astype(jnp.bfloat16)
    )
    logit_back = (
        jnp.moveaxis(grad_logit, 0, 1).reshape(row_count, head_count * REFL).astype(jnp.bfloat16)
    )
    input_term = lax.dot_general(
        proj_back, proj_weight, contract, preferred_element_type=jnp.float32
    )
    input_term = input_term + lax.dot_general(
        logit_back, beta_weight, contract, preferred_element_type=jnp.float32
    )
    grad_input = lax.psum_scatter(
        input_term.astype(jnp.bfloat16), "head", scatter_dimension=1, tiled=True
    )
    return (mixed_out, grad_input)


def solution(mesh):
    placed = (
        P("seq", "head"),
        P(None, "head"),
        P(None, "head"),
        P("head"),
        P("head", None),
        P("seq", "head"),
    )
    return jax.shard_map(
        local,
        mesh=mesh,
        in_specs=placed,
        out_specs=(P("seq", "head"), P("seq", "head")),
        check_vma=False,
    )
```

profile of v0, /device:TPU:4, one launch (start us, length us, event | category | flops | bytes accessed | tf_op | source)
XLA Modules:
  0.0 1188.4 jit_solution(16306266539693993664)
XLA Ops:
  9.6 50.3 %all-gather.3.cloned.1.call-done = bf16[512,2048]{1,0:T(8,128)(2,1)} async-done(((bf16[512,256]{1,0:T(8,128)(2,1)}), bf16[512,2048]{1,0:T(8,128)(2,1)}) %all-gather.3.cloned.1.call-update) | async-done | bytes 2097168 | tf_op jit(solution)/shard_map/all_gather | solution.py:91
  81.3 159.1 %custom-call.10 = f32[2,8,1,128,128]{3,4,2,1,0:T(8,128)} custom-call(f32[2,8,1,128,128]{4,3,2,1,0:T(8,128)} %add_bitcast_fusion), custom_call_target="InvertDiagBlocksLowerTriangular" | custom-call | tf_op jit(solution)/shard_map/jvp(vmap(vmap(jit(_solve_triangular))))/triangular_solve | solution.py:27
  255.9 25.7 %while.113 = (s32[]{:T(128)}, f32[2,128,128]{2,1,0:T(8,128)S(1)}, f32[2,128,128]{2,1,0:T(8,128)S(1)}, f32[8,2,128,128]{3,2,1,0:T(8,128)}, f32[8,2,128,128]{3,2,1...) while((s32[]{:T(128)}, f32[2,128,128]{2,1,0:T(8,128)S(1)}, ...), condition=%wide.region_2.3_spmd.clone, body=%wide.region_1.0_spmd.clone.sunk | while | flops 100761600 | bytes 1967735 | solution.py:63
  282.2 280.3 %while.109 = (s32[]{:T(128)}, f32[2,128,128]{2,1,0:T(8,128)}, f32[2,128,128]{2,1,0:T(8,128)S(1)}, f32[2,128,128]{2,1,0:T(8,128)S(1)}, f32[2,128,128]{2,1,0:T(8,128)S(1)}, /*index=5*/s32[]{:T(128)}) while((s32[]{:T(128)}, f32[2,128,128]{2,1,0:T(8,128)}, f32[2,128,128]{2,1,0:T(8,128)S(1)}, f32[2,128,128]{2,1,0:T(8,128)S(1)}, ...), condition=%wide.region_4.5_spmd, body=%wide.region_3.4_spmd.sunk | while | flops 50364416 | bytes 1573001 | solution.py:112
  284.1 6.5 collective-permute-done
  293.2 6.5 collective-permute-done
  302.2 6.5 collective-permute-done
  311.3 6.5 collective-permute-done
  320.3 6.5 collective-permute-done
  329.4 6.5 collective-permute-done
  338.4 6.5 collective-permute-done
  347.4 6.5 collective-permute-done
  356.5 6.5 collective-permute-done
  365.5 6.5 collective-permute-done
  374.6 6.5 collective-permute-done
  383.6 6.5 collective-permute-done
  392.6 6.5 collective-permute-done
  401.7 6.5 collective-permute-done
  410.7 6.5 collective-permute-done
  419.8 6.5 collective-permute-done
  428.8 6.5 collective-permute-done
  437.8 6.5 collective-permute-done
  446.9 6.5 collective-permute-done
  455.9 6.5 collective-permute-done
  465.0 6.5 collective-permute-done
  474.0 6.5 collective-permute-done
  483.0 6.5 collective-permute-done
  492.1 6.5 collective-permute-done
  501.1 6.5 collective-permute-done
  510.2 6.5 collective-permute-done
  519.2 6.5 collective-permute-done
  528.2 6.5 collective-permute-done
  537.3 6.5 collective-permute-done
  546.3 6.5 collective-permute-done
  555.4 6.5 collective-permute-done
  570.5 50.5 %while.112 = (s32[]{:T(128)}, f32[2,128,128]{2,1,0:T(8,128)S(1)}, f32[8,2,64,128]{3,2,0,1:T(8,128)S(1)}, f32[8,2,128,128]{3,2,1,0:T(8,128)}, f32[8,2,128,128]{3,...) while((s32[]{:T(128)}, f32[2,128,128]{2,1,0:T(8,128)S(1)}, ...), condition=%wide.region_7.8_spmd.clone, body=%wide.region_6.7_spmd.clone.sunk | while | flops 176259072 | bytes 3156117 | solution.py:79
  633.6 117.7 %while.114 = (s32[]{:T(128)}, f32[2,128,128]{2,1,0:T(8,128)S(1)}, f32[8,2,64,128]{3,2,0,1:T(8,128)S(1)}, f32[8,2,128,128]{3,2,0,1:T(8,128)}, f32[8,2,128,128]{3,...) while((s32[]{:T(128)}, f32[2,128,128]{2,1,0:T(8,128)S(1)}, ...), condition=%wide.region_12.13_spmd.clone, body=%wide.region_11.12_spmd.clone.sunk | while | flops 352649216 | bytes 3883208 | solution.py:79
  752.1 276.2 %while.110 = (s32[]{:T(128)}, f32[2,128,128]{2,1,0:T(8,128)}, f32[2,128,128]{2,1,0:T(8,128)S(1)}, f32[2,128,128]{2,1,0:T(8,128)S(1)}, f32[2,128,128]{2,1,0:T(8,128)S(1)}, /*index=5*/s32[]{:T(128)}) while((s32[]{:T(128)}, f32[2,128,128]{2,1,0:T(8,128)}, f32[2,128,128]{2,1,0:T(8,128)S(1)}, f32[2,128,128]{2,1,0:T(8,128)S(1)}, ...), condition=%wide.region_14.15_spmd, body=%wide.region_13.14_spmd.sunk | while | flops 50364416 | bytes 1573001 | solution.py:135
  757.2 5.9 collective-permute-start.1
  784.3 5.9 collective-permute-start.1
  793.3 5.9 collective-permute-start.1
  820.5 5.9 collective-permute-start.1
  856.6 5.9 collective-permute-start.1
  883.7 5.9 collective-permute-start.1
  892.8 5.9 collective-permute-start.1
  919.9 5.9 collective-permute-start.1
  1030.9 47.4 %while.111 = (s32[]{:T(128)}, f32[2,128,128]{2,1,0:T(8,128)S(1)}, f32[2,128,128]{2,1,0:T(8,128)S(1)}, f32[8,2,128,128]{2,3,1,0:T(8,128)}, f32[8,2,128,128]{3,2,1...) while((s32[]{:T(128)}, f32[2,128,128]{2,1,0:T(8,128)S(1)}, ...), condition=%wide.region_16.17_spmd, body=%wide.region_15.16_spmd.sunk | while | flops 201359360 | bytes 2491529 | solution.py:63
  1137.2 44.4 %reduce-scatter.5.cloned.1.call-done = bf16[512,256]{1,0:T(8,128)(2,1)} async-done(((bf16[512,2048]{1,0:T(8,128)(2,1)}), bf16[512,256]{1,0:T(8,128)(2,1)}) %reduce-scatter.5.cloned.1.call-update) | async-done | bytes 262160 | tf_op jit(solution)/shard_map/reduce_scatter | solution.py:163
  (695 shorter events, 669.5 us)
Async XLA Ops:
  7.2 52.7 %all-gather.3.cloned.1.call-start = ((), (), s32[]{:S(2)}) async-start(), calls=%async_computation.2 | async-start | bytes 2359296 | tf_op jit(solution)/shard_map/all_gather | solution.py:91
  7.9 613.1 %all-gather.5.cloned.1.call-start = ((), (), s32[]{:S(2)}) async-start(), calls=%async_computation.4 | async-start | bytes 2359296 | tf_op jit(solution)/shard_map/all_gather | solution.py:92
  8.7 1128.5 %reduce-scatter.3.cloned.1.call-start = ((), (), s32[]{:S(2)}) async-start(), calls=%async_computation.3 | async-start | bytes 2359296 | tf_op jit(solution)/shard_map/reduce_scatter | solution.py:124
  282.2 8.4 collective-permute-start
  309.4 8.4 collective-permute-start
  336.5 8.4 collective-permute-start
  363.6 8.4 collective-permute-start
  372.6 8.4 collective-permute-start
  390.7 8.4 collective-permute-start
  399.8 8.4 collective-permute-start
  417.8 8.4 collective-permute-start
  426.9 8.4 collective-permute-start
  445.0 8.4 collective-permute-start
  454.0 8.4 collective-permute-start
  481.1 8.4 collective-permute-start
  508.2 8.4 collective-permute-start
  535.4 8.4 collective-permute-start
  757.2 8.4 collective-permute-start.1
  766.2 8.4 collective-permute-start.1
  775.3 8.4 collective-permute-start.1
  784.3 8.4 collective-permute-start.1
  793.3 8.4 collective-permute-start.1
  802.4 8.4 collective-permute-start.1
  811.4 8.4 collective-permute-start.1
  820.5 8.4 collective-permute-start.1
  829.5 8.4 collective-permute-start.1
  838.5 8.4 collective-permute-start.1
  847.6 8.4 collective-permute-start.1
  856.6 8.4 collective-permute-start.1
  865.7 8.4 collective-permute-start.1
  874.7 8.4 collective-permute-start.1
  883.7 8.4 collective-permute-start.1
  892.8 8.4 collective-permute-start.1
  901.8 8.4 collective-permute-start.1
  910.8 8.4 collective-permute-start.1
  919.9 8.4 collective-permute-start.1
  928.9 8.4 collective-permute-start.1
  938.0 8.4 collective-permute-start.1
  947.0 8.4 collective-permute-start.1
  956.0 8.4 collective-permute-start.1
  965.1 8.4 collective-permute-start.1
  974.1 8.4 collective-permute-start.1
  983.1 8.4 collective-permute-start.1
  992.2 8.4 collective-permute-start.1
  1001.2 8.4 collective-permute-start.1
  1010.3 8.4 collective-permute-start.1
  1019.3 8.4 collective-permute-start.1
  1095.2 86.4 %reduce-scatter.5.cloned.1.call-start = ((), (), s32[]{:S(2)}) async-start(), calls=%async_computation.5 | async-start | bytes 2359296 | tf_op jit(solution)/shard_map/reduce_scatter | solution.py:163
  (122 other events, 2185.0 us)
Sparse Core Ops, SparseCore 0:
  9.7 50.0 all-gather.2
  61.6 47.7 all-gather.4
  1095.3 41.8 reduce-scatter.2
  1140.2 41.3 reduce-scatter.4
where the time goes:
time: 1200 us; the launch traced here: 1190 us
  waiting for transfers between devices  377 us (31%)
  matrix products  306 us (26%)
  starting transfers between devices  238 us (20%)
  other arithmetic  181 us (15%)
  local copies, waits for them, and re-layouts  68.9 us (6%)
  between operations  14.7 us (1%)
    ppermute x62, waiting for transfers between devices, passed_along(): return lax.ppermute(shard, axis, pairs)  278 us
    dot_general x240, matrix products, product(): return jnp.matmul(left, right, precision=HIGHEST)  271 us
    ppermute x62, starting transfers between devices, passed_along(): return lax.ppermute(shard, axis, pairs)  237 us
    another operation x3, other arithmetic, solve_lower(): jax.scipy.linalg.solve_triangular(matrix, target, lower=True, unit_diagon...  162 us
    all_gather x1, waiting for transfers between devices, local(): hidden_part = lax.all_gather(hidden_in, 'head', axis=1, tiled=True)  50.3 us
    reduce_scatter x1, waiting for transfers between devices, local(): lax.psum_scatter(input_term.astype(jnp.bfloat16), 'head', scatter_dimensi...  44.4 us
  transfers between devices with their start and end apart: 66, of which 65 were waited for; matrix products, arithmetic and copies ran while one was open for 27% of the time, Pallas kernels for 0%

commit v1 on v0

--- a/solution.py
+++ b/solution.py
@@ -88,8 +88,11 @@
     head_count = norm_gain.shape[0] // DK
     head_width = proj_weight.shape[1] // head_count
     contract = (((1,), (1,)), ((), ()))
-    hidden_part = lax.all_gather(hidden_in, "head", axis=1, tiled=True)
-    cot_part = lax.all_gather(cotangent, "head", axis=1, tiled=True)
+    hidden_part, cot_part = jnp.split(
+        lax.all_gather(jnp.concatenate([hidden_in, cotangent], axis=0), "head", axis=1, tiled=True),
+        [hidden_in.shape[0]],
+        axis=0,
+    )
     projected = jnp.dot(hidden_part, proj_weight, preferred_element_type=jnp.float32)
     beta_logits = jnp.dot(hidden_part, beta_weight, preferred_element_type=jnp.float32)
     dnormed = lax.dot_general(cot_part, out_weight, contract, preferred_element_type=jnp.float32)

time: 1200 us -> 1290 us (1.075)
  waiting for transfers between devices: 377 us -> 435 us
  matrix products: 306 us -> 341 us
    reduce_scatter x1, waiting for transfers between devices: 2.99 us -> 44.1 us  [local(): lax.psum_scatter(mixed_terms.astype(jnp.bfloat16), 'head', scatter_dimens...]
    dot_general x240, matrix products: 271 us -> 308 us  [product(): return jnp.matmul(left, right, precision=HIGHEST)]
    all_gather x2 -> x1, waiting for transfers between devices: 50.3 us -> 64.9 us  [local(): lax.all_gather(jnp.concatenate([hidden_in, cotangent], axis=0), 'head', a...]
  transfers between devices with their start and end apart: 66 -> 65, of which waited for: 65 -> 65; matrix products, arithmetic and copies ran while one was open for 27% -> 0% of each run, Pallas kernels for 0% -> 0%
where the time goes in v1:
time: 1290 us; the launch traced here: 1280 us
  waiting for transfers between devices  435 us (34%)
  matrix products  341 us (26%)
  starting transfers between devices  238 us (18%)
  other arithmetic  186 us (14%)
  local copies, waits for them, and re-layouts  58.3 us (5%)
  between operations  14.7 us (1%)
    dot_general x240, matrix products, product(): return jnp.matmul(left, right, precision=HIGHEST)  308 us
    ppermute x62, waiting for transfers between devices, passed_along(): return lax.ppermute(shard, axis, pairs)  288 us
    ppermute x62, starting transfers between devices, passed_along(): return lax.ppermute(shard, axis, pairs)  237 us
    another operation x3, other arithmetic, solve_lower(): jax.scipy.linalg.solve_triangular(matrix, target, lower=True, unit_diagon...  161 us
    all_gather x1, waiting for transfers between devices, local(): lax.all_gather(jnp.concatenate([hidden_in, cotangent], axis=0), 'head', a...  64.9 us
    reduce_scatter x1, waiting for transfers between devices, local(): lax.psum_scatter(mixed_terms.astype(jnp.bfloat16), 'head', scatter_dimens...  44.1 us
    reduce_scatter x1, waiting for transfers between devices, local(): lax.psum_scatter(input_term.astype(jnp.bfloat16), 'head', scatter_dimensi...  38.4 us
  transfers between devices with their start and end apart: 65, of which 65 were waited for; matrix products, arithmetic and copies ran while one was open for 0% of the time, Pallas kernels for 0%

profile of v1, /device:TPU:4, one launch (start us, length us, event | category | flops | bytes accessed | tf_op | source)
XLA Modules:
  0.0 1275.5 jit_solution(1442833844091506605)
XLA Ops:
  10.1 64.9 %all-gather.2.cloned.1.call-done = bf16[1024,2048]{1,0:T(8,128)(2,1)} async-done(((bf16[1024,256]{1,0:T(8,128)(2,1)}), bf16[1024,2048]{1,0:T(8,128)(2,1)}) %all-gather.2.cloned.1.call-update) | async-done | bytes 4194320 | tf_op jit(solution)/shard_map/all_gather | solution.py:92
  95.4 158.6 %custom-call.10 = f32[2,8,1,128,128]{3,4,2,1,0:T(8,128)} custom-call(f32[2,8,1,128,128]{4,3,2,1,0:T(8,128)} %add_bitcast_fusion), custom_call_target="InvertDiagBlocksLowerTriangular" | custom-call | tf_op jit(solution)/shard_map/jvp(vmap(vmap(jit(_solve_triangular))))/triangular_solve | solution.py:27
  272.8 18.0 %while.113 = (s32[]{:T(128)}, f32[2,128,128]{2,1,0:T(8,128)S(1)}, f32[2,128,128]{2,1,0:T(8,128)S(1)}, f32[8,2,128,128]{3,2,1,0:T(8,128)}, f32[8,2,128,128]{3,2,1...) while((s32[]{:T(128)}, f32[2,128,128]{2,1,0:T(8,128)S(1)}, ...), condition=%wide.region_2.3_spmd.clone, body=%wide.region_1.0_spmd.clone.sunk | while | flops 100761600 | bytes 1967724 | solution.py:63
  292.2 326.4 %while.109 = (s32[]{:T(128)}, f32[2,128,128]{2,1,0:T(8,128)}, f32[2,128,128]{2,1,0:T(8,128)}, f32[2,128,128]{2,1,0:T(8,128)S(1)}, f32[2,128,128]{2,1,0:T(8,128)S(1)}, /*index=5*/s32[]{:T(128)}) while((s32[]{:T(128)}, f32[2,128,128]{2,1,0:T(8,128)}, f32[2,128,128]{2,1,0:T(8,128)}, f32[2,128,128]{2,1,0:T(8,128)S(1)}, ...), condition=%wide.region_4.5_spmd, body=%wide.region_3.4_spmd.sunk | while | flops 50364416 | bytes 1048685 | solution.py:115
  294.1 6.8 collective-permute-done
  304.6 6.8 collective-permute-done
  315.2 6.8 collective-permute-done
  325.7 6.8 collective-permute-done
  336.2 6.8 collective-permute-done
  346.8 6.8 collective-permute-done
  357.3 6.8 collective-permute-done
  367.8 6.8 collective-permute-done
  378.4 6.8 collective-permute-done
  388.9 6.8 collective-permute-done
  399.4 6.8 collective-permute-done
  409.9 6.8 collective-permute-done
  420.5 6.8 collective-permute-done
  431.0 6.8 collective-permute-done
  441.5 6.8 collective-permute-done
  452.1 6.8 collective-permute-done
  462.6 6.8 collective-permute-done
  473.1 6.8 collective-permute-done
  483.7 6.8 collective-permute-done
  494.2 6.8 collective-permute-done
  504.7 6.8 collective-permute-done
  515.3 6.8 collective-permute-done
  525.8 6.8 collective-permute-done
  536.3 6.8 collective-permute-done
  546.8 6.8 collective-permute-done
  557.4 6.8 collective-permute-done
  567.9 6.8 collective-permute-done
  578.4 6.8 collective-permute-done
  589.0 6.8 collective-permute-done
  599.5 6.8 collective-permute-done
  610.0 6.8 collective-permute-done
  629.7 50.6 %while.112 = (s32[]{:T(128)}, f32[2,128,128]{2,1,0:T(8,128)S(1)}, f32[8,2,64,128]{3,2,0,1:T(8,128)S(1)}, f32[8,2,128,128]{3,2,1,0:T(8,128)}, f32[8,2,128,128]{3,...) while((s32[]{:T(128)}, f32[2,128,128]{2,1,0:T(8,128)S(1)}, ...), condition=%wide.region_7.8_spmd.clone, body=%wide.region_6.7_spmd.clone.sunk | while | flops 176259072 | bytes 3157125 | solution.py:79
  691.0 117.9 %while.114 = (s32[]{:T(128)}, f32[2,128,128]{2,1,0:T(8,128)S(1)}, f32[8,2,64,128]{3,2,0,1:T(8,128)S(1)}, f32[8,2,128,128]{3,2,0,1:T(8,128)}, f32[8,2,128,128]{3,...) while((s32[]{:T(128)}, f32[2,128,128]{2,1,0:T(8,128)S(1)}, ...), condition=%wide.region_12.13_spmd.clone, body=%wide.region_11.12_spmd.clone.sunk | while | flops 352649216 | bytes 3883200 | solution.py:79
  809.7 276.3 %while.110 = (s32[]{:T(128)}, f32[2,128,128]{2,1,0:T(8,128)}, f32[2,128,128]{2,1,0:T(8,128)S(1)}, f32[2,128,128]{2,1,0:T(8,128)S(1)}, f32[2,128,128]{2,1,0:T(8,128)S(1)}, /*index=5*/s32[]{:T(128)}) while((s32[]{:T(128)}, f32[2,128,128]{2,1,0:T(8,128)}, f32[2,128,128]{2,1,0:T(8,128)S(1)}, f32[2,128,128]{2,1,0:T(8,128)S(1)}, ...), condition=%wide.region_14.15_spmd, body=%wide.region_13.14_spmd.sunk | while | flops 50364416 | bytes 1573001 | solution.py:138
  814.7 5.9 collective-permute-start.1
  841.9 5.9 collective-permute-start.1
  869.0 5.9 collective-permute-start.1
  896.1 5.9 collective-permute-start.1
  923.2 5.9 collective-permute-start.1
  950.3 5.9 collective-permute-start.1
  959.4 5.9 collective-permute-start.1
  1088.5 47.7 %while.111 = (s32[]{:T(128)}, f32[2,128,128]{2,1,0:T(8,128)S(1)}, f32[2,128,128]{2,1,0:T(8,128)S(1)}, f32[8,2,128,128]{2,3,1,0:T(8,128)}, f32[8,2,128,128]{3,2,1...) while((s32[]{:T(128)}, f32[2,128,128]{2,1,0:T(8,128)S(1)}, ...), condition=%wide.region_16.17_spmd, body=%wide.region_15.16_spmd.sunk | while | flops 201359360 | bytes 2491521 | solution.py:63
  1186.3 38.4 %reduce-scatter.5.cloned.1.call-done = bf16[512,256]{1,0:T(8,128)(2,1)} async-done(((bf16[512,2048]{1,0:T(8,128)(2,1)}), bf16[512,256]{1,0:T(8,128)(2,1)}) %reduce-scatter.5.cloned.1.call-update) | async-done | bytes 262160 | tf_op jit(solution)/shard_map/reduce_scatter | solution.py:166
  1224.6 44.1 %reduce-scatter.3.cloned.1.call-done = bf16[512,256]{1,0:T(8,128)(2,1)} async-done(((bf16[512,2048]{1,0:T(8,128)(2,1)}), bf16[512,256]{1,0:T(8,128)(2,1)}) %reduce-scatter.3.cloned.1.call-update) | async-done | bytes 262160 | tf_op jit(solution)/shard_map/reduce_scatter | solution.py:127
  (625 shorter events, 700.8 us)
Async XLA Ops:
  7.2 67.8 %all-gather.2.cloned.1.call-start = ((), (), s32[]{:S(2)}) async-start(), calls=%async_computation.2 | async-start | bytes 4718592 | tf_op jit(solution)/shard_map/all_gather | solution.py:92
  9.2 1215.4 %reduce-scatter.5.cloned.1.call-start = ((), (), s32[]{:S(2)}) async-start(), calls=%async_computation.4 | async-start | bytes 2359296 | tf_op jit(solution)/shard_map/reduce_scatter | solution.py:166
  292.2 8.7 collective-permute-start
  302.7 8.7 collective-permute-start
  313.3 8.7 collective-permute-start
  323.8 8.7 collective-permute-start
  334.3 8.7 collective-permute-start
  344.8 8.7 collective-permute-start
  355.4 8.7 collective-permute-start
  365.9 8.7 collective-permute-start
  376.4 8.7 collective-permute-start
  387.0 8.7 collective-permute-start
  397.5 8.7 collective-permute-start
  408.0 8.7 collective-permute-start
  418.6 8.7 collective-permute-start
  429.1 8.7 collective-permute-start
  439.6 8.7 collective-permute-start
  450.2 8.7 collective-permute-start
  460.7 8.7 collective-permute-start
  471.2 8.7 collective-permute-start
  481.7 8.7 collective-permute-start
  492.3 8.7 collective-permute-start
  502.8 8.7 collective-permute-start
  513.3 8.7 collective-permute-start
  523.9 8.7 collective-permute-start
  534.4 8.7 collective-permute-start
  544.9 8.7 collective-permute-start
  555.5 8.7 collective-permute-start
  566.0 8.7 collective-permute-start
  576.5 8.7 collective-permute-start
  587.0 8.7 collective-permute-start
  597.6 8.7 collective-permute-start
  608.1 8.7 collective-permute-start
  814.7 8.4 collective-permute-start.1
  823.8 8.4 collective-permute-start.1
  832.8 8.4 collective-permute-start.1
  841.9 8.4 collective-permute-start.1
  850.9 8.4 collective-permute-start.1
  859.9 8.4 collective-permute-start.1
  869.0 8.4 collective-permute-start.1
  887.1 8.4 collective-permute-start.1
  896.1 8.4 collective-permute-start.1
  914.2 8.4 collective-permute-start.1
  923.2 8.4 collective-permute-start.1
  941.3 8.4 collective-permute-start.1
  950.3 8.4 collective-permute-start.1
  959.4 8.4 collective-permute-start.1
  1183.1 85.6 %reduce-scatter.3.cloned.1.call-start = ((), (), s32[]{:S(2)}) async-start(), calls=%async_computation.3 | async-start | bytes 2359296 | tf_op jit(solution)/shard_map/reduce_scatter | solution.py:127
  (87 other events, 1521.6 us)
Sparse Core Ops, SparseCore 0:
  9.7 65.2 all-gather.1
  1183.2 41.3 reduce-scatter.4
  1227.8 40.9 reduce-scatter.2
